TPU v7x, 32 devices: a whole 2x2x4 slice. The times are simulated.
32 devices in a mesh: parts: 2 (over x), tensor: 16 (over z, y, core).
Axes of the slice: x: 2, y: 2, z: 4, core: 2. Of those that a mesh axis runs over, the one named last changes fastest.
Arguments:
- layer_input: bfloat16 [32768, 4096], P(('parts', 'tensor')), parts along dimension 0, may hold values from -6 to 6
- down_grad: bfloat16 [32768, 4096], P(('parts', 'tensor')), parts along dimension 0, may hold values from -6 to 6
- up_grad: bfloat16 [32768, 14336], P('parts', 'tensor'), parts along dimension 0, may hold values from -6 to 6
- hidden: bfloat16 [32768, 14336], P('parts', 'tensor'), parts along dimension 0, may hold values from -6 to 6
- proj_model: bfloat16 [4096, 128], replicated, may hold values from -0.09375 to 0.09375
- proj_hidden: bfloat16 [14336, 128], P('tensor'), may hold values from -1 to 1
- assignment: int32 [64], P('parts'), parts along dimension 0, may hold values from 0 to 31, each once
- query_bank: bfloat16 [512, 8192], P('parts', 'tensor'), parts along dimension 0, may hold values from -6 to 6
- query_ids: int32 [512], P('parts'), parts along dimension 0, may hold values from 0 to 255, each once
Outputs:
- sketches: float32 [64, 8192], P('parts', 'tensor'), parts along dimension 0
- scores: float32 [64, 256], P('parts', 'tensor'), parts along dimension 0
There are 2 independent parts, one for each index of `parts`. A program takes and returns all parts, laid end to end along the dimension named above; an argument that names none is the same for every part. Nothing has to cross between parts.
Inputs may be any that keep to these rules, and one draw needn't show every extreme that they name: `assignment`: every document appears in exactly one slot. `query_ids`: every bank row appears in exactly one column.
All inputs are finite; a program needn't handle non-finite values.
Results may differ from a plain program's by a relative error of at most 0.008.
Values may be sent and summed in bfloat16 or wider, within the bound.
A program may use at most 192 MiB of HBM per device.

v0:
```python
import math

import jax
import jax.numpy as jnp
from jax import lax
from jax.sharding import PartitionSpec as P

SEQ = 512


def blocks(matrix):
    return matrix.reshape(matrix.shape[0] // SEQ, SEQ, matrix.shape[1])


def on_device(
    layer_input,
    down_grad,
    up_grad,
    hidden,
    proj_model,
    proj_hidden,
    assignment,
    query_bank,
    query_ids,
):
    sketch_width = proj_model.shape[1] // 2
    count_docs = up_grad.shape[0] // SEQ
    columns = query_bank.shape[1]
    device = lax.axis_index("tensor")
    local_up = jnp.dot(
        layer_input, proj_model[:, :sketch_width], preferred_element_type=jnp.float32
    ).astype(jnp.bfloat16)
    local_down = jnp.dot(
        down_grad, proj_model[:, sketch_width:], preferred_element_type=jnp.float32
    ).astype(jnp.bfloat16)
    every_up, every_down = (
        lax.all_gather(local_up, "tensor", axis=0, tiled=True),
        lax.all_gather(local_down, "tensor", axis=0, tiled=True),
    )
    output_up = jnp.dot(up_grad, proj_hidden[:, :sketch_width], preferred_element_type=jnp.float32)
    input_down = jnp.dot(hidden, proj_hidden[:, sketch_width:], preferred_element_type=jnp.float32)
    up_part = jnp.einsum("etr,ets->rse", blocks(output_up), blocks(every_up).astype(jnp.float32))
    down_part = jnp.einsum(
        "etr,ets->rse", blocks(every_down).astype(jnp.float32), blocks(input_down)
    )
    entry_terms = jnp.concatenate(
        [up_part.reshape(-1, count_docs), down_part.reshape(-1, count_docs)], axis=0
    )
    summed = lax.psum_scatter(entry_terms, "tensor", scatter_dimension=0, tiled=True)
    slots = jnp.take(summed, assignment, axis=1).T
    which_half = device * columns // (sketch_width * sketch_width)
    half_mask = (jnp.arange(2) == which_half).astype(jnp.float32)
    squares = jnp.sum(slots * slots, axis=1)
    totals = lax.psum(squares[:, None] * half_mask[None, :], "tensor")
    inverse = lax.rsqrt(totals / (sketch_width * sketch_width) + 1e-06)
    own_inverse = jnp.sum(inverse * half_mask[None, :], axis=1)
    sketches = slots * own_inverse[:, None]
    rounded = sketches.astype(jnp.bfloat16)
    partial_scores = jnp.dot(rounded, query_bank.T, preferred_element_type=jnp.float32)
    score_scale = 1.0 / math.sqrt(2 * sketch_width * sketch_width)
    own_columns = query_ids.shape[0] // lax.axis_size("tensor")
    bank_scores = lax.psum(partial_scores, "tensor")
    own_ids = lax.dynamic_slice_in_dim(query_ids, device * own_columns, own_columns, 0)
    raw_scores = jnp.take(bank_scores, own_ids, axis=1)
    scores = raw_scores * score_scale
    return (sketches, scores)


def solution(mesh):
    placed = (
        P(("parts", "tensor"), None),
        P(("parts", "tensor"), None),
        P("parts", "tensor"),
        P("parts", "tensor"),
        P(),
        P("tensor", None),
        P("parts"),
        P("parts", "tensor"),
        P("parts"),
    )
    return jax.shard_map(
        on_device,
        mesh=mesh,
        in_specs=placed,
        out_specs=(P("parts", "tensor"), P("parts", "tensor")),
        check_vma=False,
    )
```

profile of v0, /device:TPU:0, one launch (start us, length us, event | category | flops | bytes accessed | tf_op | source)
XLA Modules:
  0.0 260.9 jit_solution(7741574281133452797)
XLA Ops:
  7.2 0.0 copy-start
  7.2 0.0 copy-start.1
  7.2 0.0 all-gather.5.cloned.1.call-start
  7.2 7.1 %convolution_convert_fusion = bf16[1024,64]{0,1:T(8,128)(2,1)} fusion(bf16[1024,4096]{1,0:T(8,128)(2,1)} %param.10, bf16[4096,128]{1,0:T(8,128)(2,1)} %param.13), kind=kOutput, calls=%fused_computation.14 | convolution fusion | flops 536936448 | bytes 9568256 | tf_op jit(solution)/shard_map/dot_general | solution.py:33
  14.3 0.0 all-gather.5.cloned.1.call-update
  14.4 0.0 copy-start.3
  14.4 0.0 all-gather.3.cloned.1.call-start
  14.4 0.0 copy-done.1
  14.4 6.7 %convolution_convert_fusion.1 = bf16[1024,64]{0,1:T(8,128)(2,1)} fusion(bf16[1024,4096]{1,0:T(8,128)(2,1)} %param.9, bf16[4096,128]{1,0:T(8,128)(2,1)S(1)} %copy-done.1), kind=kOutput, calls=%fused_computation.15 | convolution fusion | flops 536936448 | bytes 9568256 | tf_op jit(solution)/shard_map/dot_general | solution.py:30
  21.2 0.0 all-gather.3.cloned.1.call-update
  21.2 0.0 copy-start.4
  21.2 0.0 reduce-scatter.2.cloned.1.call-start
  21.2 0.0 copy-done.3
  21.3 15.1 %fusion.22 = bf16[16384,64]{0,1:T(8,128)(2,1)} fusion(bf16[16384,896]{1,0:T(8,128)(2,1)} %param.12, bf16[896,128]{1,0:T(8,128)(2,1)S(1)} %copy-done.3), kind=kOutput, calls=%fused_computation.19 | convolution fusion | flops 1879048192 | bytes 31686656 | tf_op jit(solution)/shard_map/dot_general | solution.py:41
  36.3 0.0 copy-done.4
  36.4 13.7 %fusion.24 = bf16[16384,64]{0,1:T(8,128)(2,1)S(1)} fusion(bf16[16384,896]{1,0:T(8,128)(2,1)} %param.11, bf16[896,128]{1,0:T(8,128)(2,1)S(1)} %copy-done.4), kind=kOutput, calls=%fused_computation.21 | convolution fusion | flops 1879048192 | bytes 31686656 | tf_op jit(solution)/shard_map/dot_general | solution.py:40
  50.1 8.6 %all-gather.5.cloned.1.call-done = bf16[16384,64]{0,1:T(8,128)(2,1)} async-done(((bf16[1024,64]{0,1:T(8,128)(2,1)}), bf16[16384,64]{0,1:T(8,128)(2,1)}) %all-gather.5.cloned.1.call-update) | async-done | bytes 2097168 | tf_op jit(solution)/shard_map/all_gather | solution.py:38
  58.6 3.9 %fusion.15 = f32[64,64,32]{0,1,2:T(8,128)} fusion(bf16[8,32,8,512]{3,2,1,0:T(8,128)(2,1)} %bitcast.41, bf16[8,32,8,512]{3,2,1,0:T(8,128)(2,1)} %bitcast.40), kind=kOutput, calls=%fused_computation.13 | convolution fusion | flops 134217728 | bytes 4718592 | tf_op jit(solution)/shard_map/etr,ets->rse/dot_general | solution.py:43
  62.6 1.6 copy.28
  64.1 1.1 reshape.44
  65.3 35.8 %all-gather.3.cloned.1.call-done = bf16[16384,64]{0,1:T(8,128)(2,1)} async-done(((bf16[1024,64]{0,1:T(8,128)(2,1)}), bf16[16384,64]{0,1:T(8,128)(2,1)}) %all-gather.3.cloned.1.call-update) | async-done | bytes 2097168 | tf_op jit(solution)/shard_map/all_gather | solution.py:37
  101.1 3.3 %fusion.10 = f32[64,64,32]{0,1,2:T(8,128)} fusion(bf16[8,32,8,512]{3,2,1,0:T(8,128)(2,1)S(1)} %bitcast.39, bf16[8,32,8,512]{3,2,1,0:T(8,128)(2,1)} %bitcast.42), kind=kOutput, calls=%fused_computation.12 | convolution fusion | flops 134217728 | bytes 4718592 | tf_op jit(solution)/shard_map/etr,ets->rse/dot_general | solution.py:42
  104.4 0.0 copy-start.2
  104.4 1.6 copy.25
  106.0 0.0 copy-start.6
  106.0 0.0 copy-start.7
  106.0 0.4 reshape.41
  106.4 0.0 copy-done.2
  106.4 1.0 pad_maximum_fusion
  107.4 0.0 reduce-scatter.2.cloned.1.call-update
  107.5 0.0 copy-done.6
  107.5 0.1 compare_and_fusion
  107.6 0.0 copy-done.7
  107.6 56.2 %reduce-scatter.2.cloned.1.call-done = f32[512,32]{0,1:T(8,128)} async-done(((f32[8192,32]{0,1:T(8,128)}), f32[512,32]{0,1:T(8,128)}) %reduce-scatter.2.cloned.1.call-update) | async-done | bytes 65552 | tf_op jit(solution)/shard_map/reduce_scatter | solution.py:49
  163.8 1.5 gather_fusion
  165.3 0.2 multiply_reduce_fusion
  165.5 0.1 broadcast_multiply_fusion
  165.5 29.5 %psum.14 = f32[32,2]{0,1:T(2,128)S(1)} all-reduce(f32[32,2]{0,1:T(2,128)S(1)} %broadcast_multiply_fusion), channel_id=1, replica_groups=mesh['parts'=2,'tensor'=16] {'tensor'}, use_global_device_ids=true, to_apply=%region_2.3 | all-reduce | flops 64 | bytes 512 | tf_op jit(solution)/shard_map/psum | solution.py:54
  195.0 0.1 multiply_reduce_fusion.1
  195.1 0.1 select_multiply_fusion
  195.2 0.0 copy-done
  195.2 0.0 copy-start.5
  195.2 0.2 fusion.26
  195.4 57.7 %psum.15 = f32[32,256]{1,0:T(8,128)S(1)} all-reduce(f32[32,256]{1,0:T(8,128)S(1)} %fusion.26), channel_id=1, replica_groups=mesh['parts'=2,'tensor'=16] {'tensor'}, use_global_device_ids=true, to_apply=%region_4.5 | all-reduce | flops 8192 | bytes 65536 | tf_op jit(solution)/shard_map/psum | solution.py:62
  253.0 0.1 copy.29
  253.1 0.6 gather_fusion.1
  253.7 0.7 multiply_bitcast_fusion
  254.4 0.0 copy-done.5
  (5 shorter events, 0.0 us)
Async XLA Ops:
  7.2 188.0 %copy-start = (bf16[256,512]{1,0:T(8,128)(2,1)S(1)}, bf16[256,512]{1,0:T(8,128)(2,1)}, u32[]{:S(2)}) copy-start(bf16[256,512]{1,0:T(8,128)(2,1)} %param.16) | copy-start | bytes 786436
  7.2 7.2 %copy-start.1 = (bf16[4096,128]{1,0:T(8,128)(2,1)S(1)}, bf16[4096,128]{1,0:T(8,128)(2,1)}, u32[]{:S(2)}) copy-start(bf16[4096,128]{1,0:T(8,128)(2,1)} %param.13) | copy-start | bytes 3145732
  7.2 51.5 %all-gather.5.cloned.1.call-start = ((), (), s32[]{:S(2)}) async-start(), calls=%async_computation.2 | async-start | bytes 2228224 | tf_op jit(solution)/shard_map/all_gather | solution.py:38
  14.4 6.9 %copy-start.3 = (bf16[896,128]{1,0:T(8,128)(2,1)S(1)}, bf16[896,128]{1,0:T(8,128)(2,1)}, u32[]{:S(2)}) copy-start(bf16[896,128]{1,0:T(8,128)(2,1)} %param.14) | copy-start | bytes 688132
  14.4 86.7 %all-gather.3.cloned.1.call-start = ((), (), s32[]{:S(2)}) async-start(), calls=%async_computation.1 | async-start | bytes 2228224 | tf_op jit(solution)/shard_map/all_gather | solution.py:37
  21.2 15.2 %copy-start.4 = (bf16[896,128]{1,0:T(8,128)(2,1)S(1)}, bf16[896,128]{1,0:T(8,128)(2,1)}, u32[]{:S(2)}) copy-start(bf16[896,128]{1,0:T(8,128)(2,1)} %param.14) | copy-start | bytes 688132
  21.2 142.6 %reduce-scatter.2.cloned.1.call-start = ((), (), s32[]{:S(2)}) async-start(), calls=%async_computation.3 | async-start | bytes 1114112 | tf_op jit(solution)/shard_map/reduce_scatter | solution.py:49
  104.4 2.0 copy-start.2
  106.0 1.5 copy-start.6
  106.0 1.6 copy-start.7
  195.2 59.2 %copy-start.5 = (f32[32,512]{1,0:T(8,128)}, f32[32,512]{1,0:T(8,128)S(1)}, u32[]{:S(2)}) copy-start(f32[32,512]{1,0:T(8,128)S(1)} %select_multiply_fusion) | copy-start | bytes 196612
Sparse Core Ops, SparseCore 0:
  14.5 44.1 all-gather.4
  60.8 40.1 all-gather.2
  107.6 56.1 reduce-scatter.1
where the time goes:
time: 261 us
  waiting for transfers between devices  101 us (39%)
  blocking collectives  87.2 us (33%)
  matrix products  50 us (19%)
  between operations  13.9 us (5%)
  local copies, waits for them, and re-layouts  6.85 us (3%)
    psum x1, blocking collectives, on_device(): bank_scores = lax.psum(partial_scores, 'tensor')  57.7 us
    reduce_scatter x1, waiting for transfers between devices, on_device(): lax.psum_scatter(entry_terms, 'tensor', scatter_dimension=0, tiled=True)  56.2 us
    all_gather x1, waiting for transfers between devices, on_device(): lax.all_gather(local_up, 'tensor', axis=0, tiled=True)  35.8 us
    psum x1, blocking collectives, on_device(): totals = lax.psum(squares[:, None] * half_mask[None, :], 'tensor')  29.5 us
    dot_general x1, matrix products, on_device(): jnp.dot(hidden, proj_hidden[:, sketch_width:], preferred_element_type=jnp...  15.1 us
    dot_general x1, matrix products, on_device(): jnp.dot(up_grad, proj_hidden[:, :sketch_width], preferred_element_type=jn...  13.7 us
    all_gather x1, waiting for transfers between devices, on_device(): lax.all_gather(local_down, 'tensor', axis=0, tiled=True)  8.59 us
    dot_general x1, matrix products, on_device(): jnp.dot(down_grad, proj_model[:, sketch_width:], preferred_element_type=j...  7.09 us
  transfers between devices with their start and end apart: 3, of which 3 were waited for; matrix products, arithmetic and copies ran while one was open for 16% of the time, Pallas kernels for 0%

commit v1 on v0

--- a/solution.py
+++ b/solution.py
@@ -3,6 +3,8 @@
 import jax
 import jax.numpy as jnp
 from jax import lax
+from jax.experimental import pallas as pl
+from jax.experimental.pallas import tpu as pltpu
 from jax.sharding import PartitionSpec as P
 
 SEQ = 512
@@ -66,6 +68,332 @@
     return (sketches, scores)
 
 
+AXIS = "tensor"
+RING = 8
+F32 = jnp.float32
+BF16 = jnp.bfloat16
+HIGH = lax.Precision.HIGHEST
+
+
+def lanes(shape):
+    return lax.broadcasted_iota(jnp.int32, shape, len(shape) - 1)
+
+
+def rows(shape):
+    return lax.broadcasted_iota(jnp.int32, shape, len(shape) - 2)
+
+
+def fused_kernel(
+    layer_ref, down_ref, up_ref, hidden_ref, model_ref, proj_ref, assign_ref, bank_ref, ids_ref,
+    sketches_ref, scores_ref,
+    layer_buf, down_buf, stream, factors, weights, placed_bank, pick, staged, partials, share, shares,
+    load_sem, stream_sem, factor_send, factor_recv, sketch_send, sketch_recv, share_send, share_recv,
+):
+    me = lax.axis_index(AXIS)
+    core = me % 2
+    row_y = (me // 2) % 2
+    row_z = me // 4
+    far = row_z // 2
+    near_z = row_z + far * (3 - 2 * row_z)
+    sibling = me + 1 - 2 * core
+    across = me + 2 - 4 * row_y
+    width = up_ref.shape[1]
+
+    barrier = pltpu.get_barrier_semaphore()
+
+    @pl.loop(1, 16)
+    def _(step):
+        pl.semaphore_signal(
+            barrier, inc=1, device_id={AXIS: (me + step) % 16}, device_id_type=pl.DeviceIdType.MESH
+        )
+
+    def chip_of(group):
+        p = group // 2
+        near = jnp.where(p < 2, (p + near_z) % 2, p)
+        source_z = near + far * (3 - 2 * near)
+        source_y = (row_y + group % 2) % 2
+        return source_z * 2 + source_y
+
+    def doc_of(group, u):
+        return (chip_of(group) * 2 + (core + u // 2) % 2) * 2 + u % 2
+
+    def loads(chunk):
+        at = pl.ds(chunk * 256, 256)
+        return (
+            pltpu.make_async_copy(layer_ref.at[at], layer_buf.at[at], load_sem.at[chunk, 0]),
+            pltpu.make_async_copy(down_ref.at[at], down_buf.at[at], load_sem.at[chunk, 1]),
+        )
+
+    def streams(group, u):
+        at = pl.ds(pl.multiple_of(doc_of(group, u) * SEQ, SEQ), SEQ)
+        slot = (group % (RING // 4)) * 4 + u
+        return (
+            pltpu.make_async_copy(
+                up_ref.at[at], stream.at[slot, :, pl.ds(0, width)], stream_sem.at[slot, 0]
+            ),
+            pltpu.make_async_copy(
+                hidden_ref.at[at], stream.at[slot, :, pl.ds(width, width)], stream_sem.at[slot, 1]
+            ),
+        )
+
+    def send_doc(doc, target):
+        pltpu.make_async_remote_copy(
+            src_ref=factors.at[doc],
+            dst_ref=factors.at[doc],
+            send_sem=factor_send,
+            recv_sem=factor_recv.at[doc],
+            device_id={AXIS: target},
+            device_id_type=pl.DeviceIdType.MESH,
+        ).start()
+
+    for chunk in range(4):
+        for copy in loads(chunk):
+            copy.start()
+    for group in range(RING // 4):
+        for u in range(4):
+            for copy in streams(group, u):
+                copy.start()
+
+    proj = proj_ref[...]
+    left = lanes(proj.shape) < 64
+    weights[0:width, :] = jnp.where(left, proj, jnp.zeros_like(proj))
+    weights[width : 2 * width, :] = jnp.where(left, jnp.zeros_like(proj), proj)
+
+    left256 = lanes((256, 128)) < 64
+    for chunk in range(4):
+        for copy in loads(chunk):
+            copy.wait()
+        at = pl.ds(chunk * 256, 256)
+        ups = jnp.dot(layer_buf[at, :], model_ref[...], preferred_element_type=F32)
+        downs = jnp.dot(down_buf[at, :], model_ref[...], preferred_element_type=F32)
+        doc = me * 2 + chunk // 2
+        factors[doc, pl.ds((chunk % 2) * 256, 256), :] = jnp.where(left256, ups, downs).astype(BF16)
+        if chunk == 1:
+            pl.semaphore_wait(barrier, 15)
+        if chunk % 2 == 1:
+            send_doc(doc, across)
+            send_doc(doc, sibling)
+            for hop in range(1, 4):
+                near = jnp.where(hop < 2, (hop + near_z) % 2, hop)
+                other_z = near + far * (3 - 2 * near)
+                send_doc(doc, other_z * 4 + row_y * 2 + core)
+
+    ids = ids_ref[...]
+    matches = (rows((256, 256)) == ids).astype(BF16)
+    placed_bank[...] = lax.dot_general(
+        matches, bank_ref[...], (((0,), (0,)), ((), ())), preferred_element_type=F32
+    ).astype(BF16)
+
+    row_at = rows((256, 128))
+    wanted = jnp.zeros((256, 128), jnp.int32)
+    for slot in range(32):
+        wanted = jnp.where(row_at % 32 == slot, assign_ref[slot], wanted)
+    lane_at = lanes((256, 128))
+    same_row = lane_at % 8 == row_at // 32
+    for d in range(2):
+        hit = jnp.logical_and(same_row, wanted == (lane_at // 8) * 2 + d)
+        pick[d] = hit.astype(F32)
+
+    def pass_on(group, u):
+        doc = doc_of(group, u)
+        pltpu.make_async_copy(factors.at[doc], factors.at[doc], factor_recv.at[doc]).wait()
+        if u < 2:
+            send_doc(doc, sibling)
+
+            @pl.when(group % 2 == 0)
+            def _():
+                send_doc(doc, across)
+
+    pass_on(0, 2)
+    pass_on(0, 3)
+
+    left512 = lanes((SEQ, 128)) < 64
+    left64 = lanes((64, 128)) < 64
+
+    @pl.loop(0, 8)
+    def _(group):
+        sums = []
+        for u in range(4):
+            for copy in streams(group, u):
+                copy.wait()
+            slot = (group % (RING // 4)) * 4 + u
+            hidden_side = jnp.dot(stream[slot], weights[...], preferred_element_type=F32).astype(BF16)
+            model_side = factors[doc_of(group, u)]
+            outer = jnp.where(left512, hidden_side, model_side)
+            inner = jnp.where(left512, model_side, hidden_side)
+            sums.append(
+                lax.dot_general(outer, inner, (((0,), (0,)), ((), ())), preferred_element_type=F32)
+            )
+
+            @pl.when(group < 8 - RING // 4)
+            def _():
+                for copy in streams(group + RING // 4, u):
+                    copy.start()
+
+            @pl.when(group < 7)
+            def _():
+                pass_on(group + 1, u)
+
+        packed = []
+        for c in range(2):
+            first, second = sums[2 * c], sums[2 * c + 1]
+            upper = jnp.where(left64, first[:64], pltpu.roll(second[:64], 64, 1))
+            lower = jnp.where(left64, pltpu.roll(first[64:], 64, 1), second[64:])
+            packed.append(jnp.concatenate([upper, lower], axis=0))
+        even = core == 0
+        first = jnp.where(even, packed[0], packed[1]).reshape(16, 8, 128)
+        second = jnp.where(even, packed[1], packed[0]).reshape(16, 8, 128)
+        staged[group] = jnp.concatenate([first, second], axis=1).astype(BF16)
+        chip = chip_of(group)
+
+        @pl.loop(1, 16)
+        def _(step):
+            target = (me + step) % 16
+            pltpu.make_async_remote_copy(
+                src_ref=staged.at[group, target],
+                dst_ref=partials.at[me, chip],
+                send_sem=sketch_send,
+                recv_sem=sketch_recv,
+                device_id={AXIS: target},
+                device_id_type=pl.DeviceIdType.MESH,
+            ).start()
+
+        partials[me, chip] = staged[group, me]
+
+    most = partials.at[pl.ds(0, 15)]
+    pltpu.make_async_copy(most, most, sketch_recv).wait()
+    total = partials[0].astype(F32)
+    for sender in range(1, 16):
+        total = total + partials[sender].astype(F32)
+    total = total.reshape(128, 128)
+    picked = [
+        jnp.dot(pick[d], total, preferred_element_type=F32, precision=HIGH) for d in range(2)
+    ]
+    left32 = lanes((32, 128)) < 64
+    tiles = []
+    for pair in range(4):
+        a0, a1 = (picked[d][pair * 64 : pair * 64 + 32] for d in range(2))
+        b0, b1 = (picked[d][pair * 64 + 32 : pair * 64 + 64] for d in range(2))
+        tiles.append(
+            jnp.where(left32, a0 + pltpu.roll(a1, 64, 1), pltpu.roll(b0, 64, 1) + b1)
+        )
+    slots = jnp.concatenate(tiles, axis=1)
+    nothing = jnp.zeros((32, slots.shape[1]), F32)
+    across_rows = (((1,), (1,)), ((), ()))
+    padded = jnp.concatenate([slots, nothing, nothing, nothing], axis=0).astype(BF16)
+    raw = lax.dot_general(placed_bank[...], padded, across_rows, preferred_element_type=F32)
+    squares = jnp.concatenate([nothing, nothing, slots * slots, nothing], axis=0)
+    norms = lax.dot_general(
+        jnp.ones((8, slots.shape[1]), F32), squares, across_rows,
+        preferred_element_type=F32, precision=HIGH,
+    )
+    raw = raw.reshape(16, 2, 8, 128)
+    second = pltpu.roll(raw[:, 1].reshape(128, 128), 32, 1).reshape(16, 8, 128)
+    share[...] = raw[:, 0] + second + norms[None]
+
+    @pl.loop(1, 16)
+    def _(step):
+        target = (me + step) % 16
+        pltpu.make_async_remote_copy(
+            src_ref=share.at[target],
+            dst_ref=shares.at[me],
+            send_sem=share_send,
+            recv_sem=share_recv,
+            device_id={AXIS: target},
+            device_id_type=pl.DeviceIdType.MESH,
+        ).start()
+
+    shares[me] = share[me]
+    most = factors.at[pl.ds(0, 30)]
+    pltpu.make_async_copy(most, most, factor_send).wait()
+    most = partials.at[pl.ds(0, 15)]
+    pltpu.make_async_copy(most, most, sketch_send).wait()
+    most = shares.at[pl.ds(0, 15)]
+    pltpu.make_async_copy(most, most, share_recv).wait()
+    halves = [jnp.sum(shares[8 * h : 8 * h + 8], axis=0) for h in range(2)]
+    inverses = [lax.rsqrt(half * (1.0 / 4096) + 1e-06) for half in halves]
+    lane8 = lanes((8, 128))
+    own = jnp.where(me >= 8, inverses[1], inverses[0])
+    first_row = (rows((8, 128)) == 0).astype(F32)
+    over_rows = (((0,), (0,)), ((), ()))
+    spread = lax.dot_general(
+        own, first_row, over_rows, preferred_element_type=F32, precision=HIGH
+    )[64:96]
+    for tile in range(4):
+        sketches_ref[:, 128 * tile : 128 * tile + 128] = tiles[tile] * spread
+    scaled = jnp.zeros((8, 128), F32)
+    for half, inverse in zip(halves, inverses):
+        moved = jnp.where(lane8 < 32, pltpu.roll(inverse, 64, 1), pltpu.roll(inverse, 96, 1))
+        scaled = scaled + half * moved
+    scaled = jnp.where(lane8 < 64, scaled * (1.0 / math.sqrt(8192)), 0.0)
+    out = jnp.zeros((32, 128), F32)
+    for b in range(2):
+        place = (lane8 == rows((8, 128)) + 8 * b).astype(F32)
+        turned = lax.dot_general(
+            scaled, place, over_rows, preferred_element_type=F32, precision=HIGH
+        )
+        out = out + turned[32 * b : 32 * b + 32]
+    scores_ref[...] = out[:, :16]
+    most = share.at[pl.ds(0, 15)]
+    pltpu.make_async_copy(most, most, share_send).wait()
+
+
+def fused(
+    layer_input, down_grad, up_grad, hidden, proj_model, proj_hidden, assignment, query_bank, query_ids
+):
+    vmem = pl.BlockSpec(memory_space=pltpu.VMEM)
+    smem = pl.BlockSpec(memory_space=pltpu.SMEM)
+    hbm = pl.BlockSpec(memory_space=pl.ANY)
+    width = up_grad.shape[1]
+    return pl.pallas_call(
+        fused_kernel,
+        out_shape=(
+            jax.ShapeDtypeStruct((32, 512), F32),
+            jax.ShapeDtypeStruct((32, 16), F32),
+        ),
+        in_specs=[hbm, hbm, hbm, hbm, vmem, vmem, smem, vmem, vmem],
+        out_specs=(vmem, vmem),
+        scratch_shapes=[
+            pltpu.VMEM(layer_input.shape, BF16),
+            pltpu.VMEM(down_grad.shape, BF16),
+            pltpu.VMEM((RING, SEQ, 2 * width), BF16),
+            pltpu.VMEM((32, SEQ, 128), BF16),
+            pltpu.VMEM((2 * width, 128), BF16),
+            pltpu.VMEM((256, 512), BF16),
+            pltpu.VMEM((2, 256, 128), F32),
+            pltpu.VMEM((8, 16, 16, 128), BF16),
+            pltpu.VMEM((16, 8, 16, 128), BF16),
+            pltpu.VMEM((16, 8, 128), F32),
+            pltpu.VMEM((16, 8, 128), F32),
+            pltpu.SemaphoreType.DMA((4, 2)),
+            pltpu.SemaphoreType.DMA((RING, 2)),
+            pltpu.SemaphoreType.DMA,
+            pltpu.SemaphoreType.DMA((32,)),
+            pltpu.SemaphoreType.DMA,
+            pltpu.SemaphoreType.DMA,
+            pltpu.SemaphoreType.DMA,
+            pltpu.SemaphoreType.DMA,
+        ],
+        compiler_params=pltpu.CompilerParams(
+            collective_id=0, has_side_effects=True, vmem_limit_bytes=56 * 1024 * 1024
+        ),
+    )(
+        layer_input, down_grad, up_grad, hidden, proj_model, proj_hidden,
+        assignment, query_bank, query_ids.reshape(1, -1),
+    )
+
+
+def choose(*arrays):
+    shapes = tuple(array.shape for array in arrays)
+    fits = (
+        (1024, 4096), (1024, 4096), (16384, 896), (16384, 896), (4096, 128), (896, 128),
+        (32,), (256, 512), (256,),
+    )
+    if lax.axis_size(AXIS) == 16 and shapes == fits:
+        return fused(*arrays)
+    return on_device(*arrays)
+
+
 def solution(mesh):
     placed = (
         P(("parts", "tensor"), None),
@@ -79,7 +407,7 @@
         P("parts"),
     )
     return jax.shard_map(
-        on_device,
+        choose,
         mesh=mesh,
         in_specs=placed,
         out_specs=(P("parts", "tensor"), P("parts", "tensor")),

time: 261 us -> 79.8 us (0.31)
  waiting for transfers between devices: 101 us -> 0 us
  blocking collectives: 87.2 us -> 0 us
  Pallas kernels: 0 us -> 76 us
  matrix products: 50 us -> 0 us
  between operations: 13.9 us -> 0.64 us
  local copies, waits for them, and re-layouts: 6.85 us -> 2.86 us
    psum x2 -> x0, blocking collectives: 87.2 us -> none  [the longest x1 57.7 us: on_device(): bank_scores = lax.psum(partial_scores, 'tensor')]
    pallas_call x0 -> x1, Pallas kernels: none -> 76 us  [fused(): pl.pallas_call(fused_kernel, out_shape=(jax.ShapeDtypeStruct((32, 512), F...]
    reduce_scatter x1 -> x0, waiting for transfers between devices: 56.2 us -> none  [on_device(): lax.psum_scatter(entry_terms, 'tensor', scatter_dimension=0, tiled=True)]
    dot_general x7 -> x0, matrix products: 50 us -> none  [the longest x1 15.1 us: on_device(): jnp.dot(hidden, proj_hidden[:, sketch_width:], preferred_element_type=jnp...]
    all_gather x2 -> x0, waiting for transfers between devices: 44.4 us -> none  [the longest x1 35.8 us: on_device(): lax.all_gather(local_up, 'tensor', axis=0, tiled=True)]
    transpose x2 -> x0, local copies, waits for them, and re-layouts: 3.17 us -> none  [the longest x1 1.61 us: on_device(): jnp.einsum('etr,ets->rse', blocks(output_up), blocks(every_up).astype(jnp...]
  transfers between devices with their start and end apart: 3 -> 0, of which waited for: 3 -> 0; matrix products, arithmetic and copies ran while one was open for 16% -> 0% of each run, Pallas kernels for 0% -> 0%
where the time goes in v1:
time: 79.8 us; the launch traced here: 79.5 us
  Pallas kernels  76 us (95%)
  local copies, waits for them, and re-layouts  2.86 us (4%)
    pallas_call x1, Pallas kernels, fused(): pl.pallas_call(fused_kernel, out_shape=(jax.ShapeDtypeStruct((32, 512), F...  76 us

profile of v1, /device:TPU:0, one launch (start us, length us, event | category | flops | bytes accessed | tf_op | source)
XLA Modules:
  0.0 79.5 jit_solution(9003891314383391803)
XLA Ops:
  0.6 76.0 %shard_map.104 = (f32[32,512]{1,0:T(8,128)}, f32[32,16]{1,0:T(8,128)}) custom-call(bf16[1024,4096]{1,0:T(8,128)(2,1)} %layer_ref.1, bf16[1024,4096]{1,0:T(8,128)(2,1)} %down_ref.1, bf16[16384,896]{1,0:T(8,128)(2,1)} %up_ref.1, bf16[16384,896]{1,0:T(8,128)(2,1)} %hidden_ref.1, bf16[4096,128]{1,0:T(8,128)(2,1)} %model_ref.1, bf16[896,128]{1,0:T(8,128)(2,1)} %proj_ref.1, ...), custom_call_target="tpu_custom_call" | custom-call | tf_op jit(solution)/shard_map/pallas_call | solution.py:348
  76.7 1.4 %copy.11 = f32[32,16]{0,1:T(8,128)} copy(f32[32,16]{1,0:T(8,128)} %get-tuple-element.3) | data formatting | bytes 4096 | tf_op jit(solution)/shard_map/pallas_call | solution.py:348
  78.1 1.5 %copy.13 = f32[32,512]{1,0:T(8,128)} copy(f32[32,512]{1,0:T(8,128)} %get-tuple-element.6) | data formatting | bytes 131072

commit v2 on v1

--- a/solution.py
+++ b/solution.py
@@ -70,6 +70,7 @@
 
 AXIS = "tensor"
 RING = 8
+UNIT = 4
 F32 = jnp.float32
 BF16 = jnp.bfloat16
 HIGH = lax.Precision.HIGHEST
@@ -118,21 +119,25 @@
         return (chip_of(group) * 2 + (core + u // 2) % 2) * 2 + u % 2
 
     def loads(chunk):
-        at = pl.ds(chunk * 256, 256)
+        at = pl.ds(chunk * SEQ, SEQ)
         return (
             pltpu.make_async_copy(layer_ref.at[at], layer_buf.at[at], load_sem.at[chunk, 0]),
             pltpu.make_async_copy(down_ref.at[at], down_buf.at[at], load_sem.at[chunk, 1]),
         )
+
+    def slot_rows(group, u, count):
+        first = ((group % (RING // 4)) * 4 + u) * SEQ
+        return pl.ds(pl.multiple_of(first, SEQ), count * SEQ)
 
     def streams(group, u):
         at = pl.ds(pl.multiple_of(doc_of(group, u) * SEQ, SEQ), SEQ)
         slot = (group % (RING // 4)) * 4 + u
         return (
             pltpu.make_async_copy(
-                up_ref.at[at], stream.at[slot, :, pl.ds(0, width)], stream_sem.at[slot, 0]
+                up_ref.at[at], stream.at[slot_rows(group, u, 1), pl.ds(0, width)], stream_sem.at[slot, 0]
             ),
             pltpu.make_async_copy(
-                hidden_ref.at[at], stream.at[slot, :, pl.ds(width, width)], stream_sem.at[slot, 1]
+                hidden_ref.at[at], stream.at[slot_rows(group, u, 1), pl.ds(width, width)], stream_sem.at[slot, 1]
             ),
         )
 
@@ -146,7 +151,7 @@
             device_id_type=pl.DeviceIdType.MESH,
         ).start()
 
-    for chunk in range(4):
+    for chunk in range(2):
         for copy in loads(chunk):
             copy.start()
     for group in range(RING // 4):
@@ -159,24 +164,23 @@
     weights[0:width, :] = jnp.where(left, proj, jnp.zeros_like(proj))
     weights[width : 2 * width, :] = jnp.where(left, jnp.zeros_like(proj), proj)
 
-    left256 = lanes((256, 128)) < 64
-    for chunk in range(4):
+    left512 = lanes((SEQ, 128)) < 64
+    for chunk in range(2):
         for copy in loads(chunk):
             copy.wait()
-        at = pl.ds(chunk * 256, 256)
+        at = pl.ds(chunk * SEQ, SEQ)
         ups = jnp.dot(layer_buf[at, :], model_ref[...], preferred_element_type=F32)
         downs = jnp.dot(down_buf[at, :], model_ref[...], preferred_element_type=F32)
-        doc = me * 2 + chunk // 2
-        factors[doc, pl.ds((chunk % 2) * 256, 256), :] = jnp.where(left256, ups, downs).astype(BF16)
-        if chunk == 1:
+        doc = me * 2 + chunk
+        factors[doc] = jnp.where(left512, ups, downs).astype(BF16)
+        if chunk == 0:
             pl.semaphore_wait(barrier, 15)
-        if chunk % 2 == 1:
-            send_doc(doc, across)
-            send_doc(doc, sibling)
-            for hop in range(1, 4):
-                near = jnp.where(hop < 2, (hop + near_z) % 2, hop)
-                other_z = near + far * (3 - 2 * near)
-                send_doc(doc, other_z * 4 + row_y * 2 + core)
+        send_doc(doc, across)
+        send_doc(doc, sibling)
+        for hop in range(1, 4):
+            near = jnp.where(hop < 2, (hop + near_z) % 2, hop)
+            other_z = near + far * (3 - 2 * near)
+            send_doc(doc, other_z * 4 + row_y * 2 + core)
 
     ids = ids_ref[...]
     matches = (rows((256, 256)) == ids).astype(BF16)
@@ -207,32 +211,37 @@
     pass_on(0, 2)
     pass_on(0, 3)
 
-    left512 = lanes((SEQ, 128)) < 64
     left64 = lanes((64, 128)) < 64
 
     @pl.loop(0, 8)
     def _(group):
         sums = []
-        for u in range(4):
-            for copy in streams(group, u):
-                copy.wait()
-            slot = (group % (RING // 4)) * 4 + u
-            hidden_side = jnp.dot(stream[slot], weights[...], preferred_element_type=F32).astype(BF16)
-            model_side = factors[doc_of(group, u)]
-            outer = jnp.where(left512, hidden_side, model_side)
-            inner = jnp.where(left512, model_side, hidden_side)
-            sums.append(
-                lax.dot_general(outer, inner, (((0,), (0,)), ((), ())), preferred_element_type=F32)
-            )
+        for base in range(0, 4, UNIT):
+            for u in range(base, base + UNIT):
+                for copy in streams(group, u):
+                    copy.wait()
+            hidden_sides = jnp.dot(
+                stream[slot_rows(group, base, UNIT), :], weights[...], preferred_element_type=F32
+            ).astype(BF16)
+            for u in range(base, base + UNIT):
+                hidden_side = hidden_sides[(u - base) * SEQ : (u - base + 1) * SEQ]
+                model_side = factors[doc_of(group, u)]
+                outer = jnp.where(left512, hidden_side, model_side)
+                inner = jnp.where(left512, model_side, hidden_side)
+                sums.append(
+                    lax.dot_general(outer, inner, (((0,), (0,)), ((), ())), preferred_element_type=F32)
+                )
 
             @pl.when(group < 8 - RING // 4)
             def _():
-                for copy in streams(group + RING // 4, u):
-                    copy.start()
+                for u in range(base, base + UNIT):
+                    for copy in streams(group + RING // 4, u):
+                        copy.start()
 
             @pl.when(group < 7)
             def _():
-                pass_on(group + 1, u)
+                for u in range(base, base + UNIT):
+                    pass_on(group + 1, u)
 
         packed = []
         for c in range(2):
@@ -356,7 +365,7 @@
         scratch_shapes=[
             pltpu.VMEM(layer_input.shape, BF16),
             pltpu.VMEM(down_grad.shape, BF16),
-            pltpu.VMEM((RING, SEQ, 2 * width), BF16),
+            pltpu.VMEM((RING * SEQ, 2 * width), BF16),
             pltpu.VMEM((32, SEQ, 128), BF16),
             pltpu.VMEM((2 * width, 128), BF16),
             pltpu.VMEM((256, 512), BF16),
@@ -365,7 +374,7 @@
             pltpu.VMEM((16, 8, 16, 128), BF16),
             pltpu.VMEM((16, 8, 128), F32),
             pltpu.VMEM((16, 8, 128), F32),
-            pltpu.SemaphoreType.DMA((4, 2)),
+            pltpu.SemaphoreType.DMA((2, 2)),
             pltpu.SemaphoreType.DMA((RING, 2)),
             pltpu.SemaphoreType.DMA,
             pltpu.SemaphoreType.DMA((32,)),

time: 79.8 us -> 76 us (0.952)
  Pallas kernels: 76 us -> 72.3 us
    pallas_call x1, Pallas kernels: 76 us -> 72.3 us  [fused(): pl.pallas_call(fused_kernel, out_shape=(jax.ShapeDtypeStruct((32, 512), F...]
where the time goes in v2:
time: 76 us; the launch traced here: 75.8 us
  Pallas kernels  72.3 us (95%)
  local copies, waits for them, and re-layouts  2.86 us (4%)
    pallas_call x1, Pallas kernels, fused(): pl.pallas_call(fused_kernel, out_shape=(jax.ShapeDtypeStruct((32, 512), F...  72.3 us

profile of v2, /device:TPU:0, one launch (start us, length us, event | category | flops | bytes accessed | tf_op | source)
XLA Modules:
  0.0 75.8 jit_solution(3968706496937573066)
XLA Ops:
  0.6 72.3 %shard_map.104 = (f32[32,512]{1,0:T(8,128)}, f32[32,16]{1,0:T(8,128)}) custom-call(bf16[1024,4096]{1,0:T(8,128)(2,1)} %layer_ref.1, bf16[1024,4096]{1,0:T(8,128)(2,1)} %down_ref.1, bf16[16384,896]{1,0:T(8,128)(2,1)} %up_ref.1, bf16[16384,896]{1,0:T(8,128)(2,1)} %hidden_ref.1, bf16[4096,128]{1,0:T(8,128)(2,1)} %model_ref.1, bf16[896,128]{1,0:T(8,128)(2,1)} %proj_ref.1, ...), custom_call_target="tpu_custom_call" | custom-call | tf_op jit(solution)/shard_map/pallas_call | solution.py:357
  72.9 1.4 %copy.11 = f32[32,16]{0,1:T(8,128)} copy(f32[32,16]{1,0:T(8,128)} %get-tuple-element.3) | data formatting | bytes 4096 | tf_op jit(solution)/shard_map/pallas_call | solution.py:357
  74.3 1.5 %copy.13 = f32[32,512]{1,0:T(8,128)} copy(f32[32,512]{1,0:T(8,128)} %get-tuple-element.6) | data formatting | bytes 131072
